TPU v7x, 32 devices: a whole 2x2x4 slice. The times are simulated.
32 devices in a mesh: row: 4 (over y, core), col: 8 (over z, x).
Axes of the slice: x: 2, y: 2, z: 4, core: 2. Of those that a mesh axis runs over, the one named last changes fastest.
Arguments:
- probes: bfloat16 [4, 8192, 256], P(None, ('row', 'col')), may hold values from -6 to 6
- points: bfloat16 [16, 4, 8192], P(None, None, ('row', 'col')), may hold values from -8 to 8
- leaf_skeleton: int32 [64, 64], P(('row', 'col')), may hold values from 0 to 127, as said below
- skeleton_one: int32 [32, 64], P(('row', 'col')), may hold values from 0 to 127, as said below
- skeleton_two: int32 [16, 64], P('row'), may hold values from 0 to 127, as said below
- skeleton_three: int32 [8, 64], P('row'), may hold values from 0 to 127, as said below
Outputs:
- leaf_interp: float32 [64, 128, 64], P(('row', 'col'))
- upper_interp: float32 [3, 32, 128, 64], P(None, ('row', 'col'))
- top_state: float32 [2, 32, 64, 256], P(None, ('row', 'col'))
Inputs may be any that keep to these rules, and one draw needn't show every extreme that they name: `leaf_skeleton`: each row names 64 different rows of its leaf, in ascending order. `skeleton_one`: each row names 64 different rows of the node's stacked child skeletons, in ascending order. `skeleton_two`: each row names 64 different rows of the node's stacked child skeletons, in ascending order. `skeleton_three`: each row names 64 different rows of the node's stacked child skeletons, in ascending order.
All inputs are finite; a program needn't handle non-finite values.
Results may differ from a plain program's by a relative error of at most 0.0059.
Values may be sent and summed in bfloat16 or wider, within the bound.
No kernel may reach another device: no remote copies, remote signals or barrier semaphores. Data moves between devices by JAX's collectives and lax.ppermute only.
A program may use at most 64 MiB of HBM per device.

v0:
```python
from functools import partial
import math

import jax
import jax.numpy as jnp
from jax import lax
from jax.sharding import PartitionSpec as P

LEAF = 128


exact_mode = lax.Precision.HIGHEST


def swapped(value, axis, bit):
    return lax.ppermute(value, axis, [(i, i ^ 1 << bit) for i in range(lax.axis_size(axis))])


def couple(row_feats, col_feats, kernel_gain):
    cross = jnp.dot(row_feats.T, col_feats, precision=exact_mode)
    row_sq = jnp.sum(row_feats * row_feats, axis=0)
    col_sq = jnp.sum(col_feats * col_feats, axis=0)
    feat_count = row_feats.shape[0]
    return kernel_gain * jnp.exp(
        (2.0 * cross - row_sq[:, None] - col_sq[None, :]) / (2.0 * feat_count)
    )


def interpolate(stacked, chosen):
    skeleton = jnp.take(stacked, chosen, axis=0)
    gram_mat = jnp.dot(skeleton, skeleton.T, precision=exact_mode)
    damping = 0.05 * jnp.sum(skeleton * skeleton) / chosen.shape[0] + 1e-05
    factor = jnp.linalg.cholesky(gram_mat + damping * jnp.eye(chosen.shape[0], dtype=stacked.dtype))
    cross_mat = jnp.dot(stacked, skeleton.T, precision=exact_mode)
    solved = jax.scipy.linalg.cho_solve((factor, True), cross_mat.T)
    return (solved.T, skeleton)


def leaf_level(leaf_rows, leaf_probes, coords, chosen):
    interp, skeleton = interpolate(leaf_rows, chosen)
    reduced = jnp.dot(interp.T, leaf_probes.astype(interp.dtype), precision=exact_mode)
    picked = jnp.take(coords, chosen, axis=1).astype(jnp.float32)
    return (interp, (skeleton, reduced, picked))


def merge_pair(first_child, second_child, chosen, kernel_gain):
    first_samples, first_reduced, first_points = first_child
    second_samples, second_reduced, second_points = second_child
    upper_rows = first_samples - jnp.dot(
        couple(first_points, second_points, kernel_gain), second_reduced, precision=exact_mode
    )
    lower_rows = second_samples - jnp.dot(
        couple(second_points, first_points, kernel_gain), first_reduced, precision=exact_mode
    )
    stacked = jnp.concatenate([upper_rows, lower_rows], axis=0)
    interp, skeleton = interpolate(stacked, chosen)
    reduced = jnp.dot(
        interp.T, jnp.concatenate([first_reduced, second_reduced], axis=0), precision=exact_mode
    )
    joined = jnp.take(jnp.concatenate([first_points, second_points], axis=1), chosen, axis=1)
    return (interp, (skeleton, reduced, joined))


def take_first(values):
    return values[0]


def take_second(values):
    return values[1]


def local(probes, points, leaf_skeleton, skeleton_one, skeleton_two, skeleton_three):
    feat_count = points.shape[0]
    own_rows = probes.shape[1]
    row_count = lax.axis_size("row")
    col_count = lax.axis_size("col")
    row_pos = lax.axis_index("row")
    col_pos = lax.axis_index("col")
    row_span = own_rows * col_count
    extent = row_span * row_count
    kernel_gain = 16.0 / math.sqrt(4 * extent)
    probe_cols = lax.all_gather(probes, "row", axis=1, tiled=True).reshape(
        4 * row_count * own_rows, -1
    )
    row_coords = lax.all_gather(points[:, 0], "col", axis=1, tiled=True)
    col_coords = lax.all_gather(points, "row", axis=2, tiled=True).reshape(
        feat_count, 4 * row_count * own_rows
    )
    col_wide = col_coords.astype(jnp.float32)
    col_sq = jnp.sum(col_wide * col_wide, axis=0)
    row_leaf = (row_pos * row_span + jnp.arange(row_span, dtype=jnp.int32)) // LEAF
    quarter_len = row_count * own_rows
    offsets = jnp.arange(4 * quarter_len, dtype=jnp.int32)
    quarter = offsets // quarter_len
    within = offsets % quarter_len
    col_leaf = (
        quarter * extent + within // own_rows * row_span + col_pos * own_rows + within % own_rows
    ) // LEAF
    height = 512

    def one_block(first_row):
        coords = lax.dynamic_slice_in_dim(row_coords, first_row, height, 1)
        leaves = lax.dynamic_slice_in_dim(row_leaf, first_row, height, 0)
        cross = lax.dot_general(
            coords, col_coords, (((0,), (0,)), ((), ())), preferred_element_type=jnp.float32
        )
        row_wide = coords.astype(jnp.float32)
        row_sq = jnp.sum(row_wide * row_wide, axis=0)
        kernel_tile = kernel_gain * jnp.exp(
            (2.0 * cross - row_sq[:, None] - col_sq[None, :]) / (2.0 * feat_count)
        )
        kernel_tile = jnp.where(leaves[:, None] == col_leaf[None, :], 0.0, kernel_tile).astype(
            jnp.bfloat16
        )
        return jnp.dot(kernel_tile, probe_cols, preferred_element_type=jnp.float32)

    starts = jnp.arange(own_rows * lax.axis_size("col") // height, dtype=jnp.int32) * height
    owned = lax.psum_scatter(
        lax.map(one_block, starts).reshape(own_rows * lax.axis_size("col"), -1),
        "col",
        scatter_dimension=0,
        tiled=True,
    )
    leaf_count = own_rows // LEAF
    leaf_rows = owned.reshape(leaf_count, LEAF, -1)
    leaf_probes = probes[0].reshape(leaf_count, LEAF, -1)
    leaf_coords = points[:, 0].reshape(feat_count, leaf_count, LEAF).transpose(1, 0, 2)
    leaf_interp, carried = jax.vmap(leaf_level)(leaf_rows, leaf_probes, leaf_coords, leaf_skeleton)
    first_child = jax.tree.map(take_first, carried)
    second_child = jax.tree.map(take_second, carried)
    interp_one, carried = merge_pair(first_child, second_child, skeleton_one[0], kernel_gain)
    upper_list = [interp_one]
    for bit_num in range(2):
        partner = swapped((carried[0], carried[1], carried[2]), "col", bit_num)
        mine_first = col_pos >> bit_num & 1 == 0
        first_child = jax.tree.map(partial(jnp.where, mine_first), carried, partner)
        second_child = jax.tree.map(partial(jnp.where, mine_first), partner, carried)
        table_rows = skeleton_two if bit_num == 0 else skeleton_three
        chosen = lax.dynamic_index_in_dim(table_rows, col_pos // (2 << bit_num), 0, keepdims=False)
        interp_up, carried = merge_pair(first_child, second_child, chosen, kernel_gain)
        upper_list.append(interp_up)
    upper_interp = jnp.stack(upper_list)[:, None]
    top_state = jnp.stack([carried[0], carried[1]])[:, None]
    return (leaf_interp, upper_interp, top_state)


def solution(mesh):
    placed = (
        P(None, ("row", "col"), None),
        P(None, None, ("row", "col")),
        P(("row", "col"), None),
        P(("row", "col"), None),
        P("row", None),
        P("row", None),
    )
    return jax.shard_map(
        local,
        mesh=mesh,
        in_specs=placed,
        out_specs=(
            P(("row", "col"), None, None),
            P(None, ("row", "col"), None, None),
            P(None, ("row", "col"), None, None),
        ),
        check_vma=False,
    )
```

profile of v0, /device:TPU:0, one launch (start us, length us, event | category | flops | bytes accessed | tf_op | source)
XLA Modules:
  0.0 242.0 jit_solution(2204437148597688408)
XLA Ops:
  7.2 0.7 all-gather.3.cloned.1.call-update
  8.0 0.8 slice.59
  8.7 6.8 %all_gather.10 = bf16[16,4,1024]{2,1,0:T(4,128)(2,1)S(1)} all-gather(bf16[16,4,256]{2,1,0:T(4,128)(2,1)} %param.16), channel_id=1, replica_groups=mesh['row'=4,'col'=8] {'row'}, dimensions={2}, use_global_device_ids=true | all-gather | bytes 163840 | tf_op jit(solution)/shard_map/all_gather | solution.py:86
  15.6 31.2 %all-gather = bf16[16,1,2048]{2,0,1:T(8,128)(2,1)S(1)} all-gather(bf16[16,1,256]{2,0,1:T(8,128)(2,1)S(1)} %copy.60), channel_id=2, replica_groups=mesh['row'=4,'col'=8] {'col'}, dimensions={2}, use_global_device_ids=true | all-gather | bytes 73728 | tf_op jit(solution)/shard_map/all_gather | solution.py:85
  46.9 32.4 %while.11 = (s32[]{:T(128)}, f32[4,512,256]{2,1,0:T(8,128)}, s32[4]{0:T(128)S(1)}, s32[2048]{0:T(1024)S(1)}, bf16[16,2048]{1,0:T(8,128)(2,1)S(1)}, /*index=5*/bf...) while((s32[]{:T(128)}, f32[4,512,256]{2,1,0:T(8,128)}, ...), condition=%wide.region_3.4_spmd.clone, body=%wide.region_1.3_spmd.clone.sunk | while | flops 1157860864 | bytes 2844863 | solution.py:119
  46.9 0.6 dynamic_slice.37
  49.6 5.4 %fusion.174 = f32[4,512,256]{2,1,0:T(8,128)} fusion(f32[4,512,256]{2,1,0:T(8,128)} %get-tuple-element.213, s32[]{:T(128)S(6)} %copy.69, bf16[4096,256]{1,0:T(8,128)(2,1)} %get-tuple-element.231, bf16[16,4096]{1,0:T(8,128)(2,1)S(1)} %get-tuple-element.229, f32[4096]{0:T(1024)S(1)} %get-tuple-element.230, f32[512]{0:T(512)S(1)} %multiply_reduce_fusion.13, ...), kind=kOutput, calls=%fused_computation.11.clone.1 | convolution fusion | flops 1157627904 | bytes 2805768 | tf_op jit(solution)/shard_map/while/body/eval_jaxpr/dot_general | solution.py:115
  55.0 0.6 dynamic_slice.37
  57.7 5.4 %fusion.174 = f32[4,512,256]{2,1,0:T(8,128)} fusion(f32[4,512,256]{2,1,0:T(8,128)} %get-tuple-element.213, s32[]{:T(128)S(6)} %copy.69, bf16[4096,256]{1,0:T(8,128)(2,1)} %get-tuple-element.231, bf16[16,4096]{1,0:T(8,128)(2,1)S(1)} %get-tuple-element.229, f32[4096]{0:T(1024)S(1)} %get-tuple-element.230, f32[512]{0:T(512)S(1)} %multiply_reduce_fusion.13, ...), kind=kOutput, calls=%fused_computation.11.clone.1 | convolution fusion | flops 1157627904 | bytes 2805768 | tf_op jit(solution)/shard_map/while/body/eval_jaxpr/dot_general | solution.py:115
  63.1 0.6 dynamic_slice.37
  65.9 5.3 %fusion.174 = f32[4,512,256]{2,1,0:T(8,128)} fusion(f32[4,512,256]{2,1,0:T(8,128)} %get-tuple-element.213, s32[]{:T(128)S(6)} %copy.69, bf16[4096,256]{1,0:T(8,128)(2,1)} %get-tuple-element.231, bf16[16,4096]{1,0:T(8,128)(2,1)S(1)} %get-tuple-element.229, f32[4096]{0:T(1024)S(1)} %get-tuple-element.230, f32[512]{0:T(512)S(1)} %multiply_reduce_fusion.13, ...), kind=kOutput, calls=%fused_computation.11.clone.1 | convolution fusion | flops 1157627904 | bytes 2805768 | tf_op jit(solution)/shard_map/while/body/eval_jaxpr/dot_general | solution.py:115
  71.2 0.6 dynamic_slice.37
  74.0 5.4 %fusion.174 = f32[4,512,256]{2,1,0:T(8,128)} fusion(f32[4,512,256]{2,1,0:T(8,128)} %get-tuple-element.213, s32[]{:T(128)S(6)} %copy.69, bf16[4096,256]{1,0:T(8,128)(2,1)} %get-tuple-element.231, bf16[16,4096]{1,0:T(8,128)(2,1)S(1)} %get-tuple-element.229, f32[4096]{0:T(1024)S(1)} %get-tuple-element.230, f32[512]{0:T(512)S(1)} %multiply_reduce_fusion.13, ...), kind=kOutput, calls=%fused_computation.11.clone.1 | convolution fusion | flops 1157627904 | bytes 2805768 | tf_op jit(solution)/shard_map/while/body/eval_jaxpr/dot_general | solution.py:115
  79.4 0.6 copy-done.1
  80.2 1.1 gather_fusion.1
  81.7 0.6 gather_fusion.3
  82.4 1.5 collective-permute-start.1
  83.9 0.7 compare_and_fusion
  85.1 0.9 slice.65
  86.5 0.6 gather_fusion.5
  87.7 5.0 %collective-permute-done.4 = f32[16,64]{0,1:T(8,128)S(1)} collective-permute-done((f32[16,64]{0,1:T(8,128)S(1)}, f32[16,64]{0,1:T(8,128)S(1)}, u32[]{:S(2)}, u32[]{:S(2)}) %collective-permute-start.4) | collective-permute-done | bytes 4128 | tf_op jit(solution)/shard_map/ppermute | solution.py:16
  92.8 55.9 %reduce-scatter.2.cloned.1.call-done = f32[256,256]{1,0:T(8,128)} async-done(((f32[2048,256]{1,0:T(8,128)}), f32[256,256]{1,0:T(8,128)}) %reduce-scatter.2.cloned.1.call-update) | async-done | bytes 262160 | tf_op jit(solution)/shard_map/reduce_scatter | solution.py:118
  148.7 1.9 gather_fusion
  150.8 1.3 fusion.120
  152.2 0.3 fusion.119
  152.6 11.7 %custom-call.18 = f32[2,64,64]{2,1,0:T(8,128)S(1)} custom-call(f32[2,64,64]{2,1,0:T(8,128)S(1)} %fusion.80), custom_call_target="Cholesky" | custom-call | tf_op jit(solution)/shard_map/vmap(jit(cholesky))/cholesky | solution.py:33
  164.6 10.0 %custom-call.19 = f32[2,1,64,64]{2,3,1,0:T(8,128)S(1)} custom-call(f32[2,1,64,64]{3,2,1,0:T(8,128)S(1)} %select_bitcast_fusion), custom_call_target="InvertDiagBlocksLowerTriangular" | custom-call | tf_op jit(solution)/shard_map/vmap(jit(_cho_solve))/triangular_solve | solution.py:35
  174.6 0.3 fusion.77
  175.8 0.7 gather_fusion.2
  176.4 0.7 multiply_reduce_fusion.5
  177.1 0.3 fusion.117
  178.3 5.8 %cholesky.106 = f32[64,64]{1,0:T(8,128)S(1)} custom-call(f32[64,64]{1,0:T(8,128)S(1)} %fusion.101), custom_call_target="Cholesky" | custom-call | tf_op jit(solution)/shard_map/jit(cholesky)/cholesky | solution.py:33
  184.2 0.6 compare_reduce_fusion.2
  184.9 0.7 fusion.84
  185.5 4.9 %custom-call.26 = f32[1,64,64]{1,2,0:T(8,128)S(1)} custom-call(f32[1,64,64]{2,1,0:T(8,128)S(1)} %fusion.84), custom_call_target="InvertDiagBlocksLowerTriangular" | custom-call | tf_op jit(solution)/shard_map/jit(_cho_solve)/triangular_solve | solution.py:35
  190.4 0.3 fusion.99
  190.8 0.2 fusion.64
  191.1 0.8 collective-permute-start.2
  192.1 1.4 collective-permute-start
  193.4 2.0 collective-permute-done.2
  195.6 0.8 collective-permute-done
  196.6 0.7 gather_fusion.4
  197.3 0.7 multiply_reduce_fusion.4
  198.0 0.3 fusion.116
  199.2 5.8 %cholesky.117 = f32[64,64]{1,0:T(8,128)S(1)} custom-call(f32[64,64]{1,0:T(8,128)S(1)} %fusion.96), custom_call_target="Cholesky" | custom-call | tf_op jit(solution)/shard_map/jit(cholesky)/cholesky | solution.py:33
  205.1 0.6 compare_reduce_fusion.1
  205.7 0.7 fusion.85
  206.4 4.9 %custom-call.27 = f32[1,64,64]{1,2,0:T(8,128)S(1)} custom-call(f32[1,64,64]{2,1,0:T(8,128)S(1)} %fusion.85), custom_call_target="InvertDiagBlocksLowerTriangular" | custom-call | tf_op jit(solution)/shard_map/jit(_cho_solve)/triangular_solve | solution.py:35
  211.3 0.3 fusion.94
  211.9 1.8 collective-permute-start.5
  213.9 0.4 collective-permute-start.3
  214.3 2.0 collective-permute-done.5
  216.5 1.8 collective-permute-done.3
  218.5 0.7 gather_fusion.6
  219.1 0.3 fusion.81
  219.4 0.7 select_bitcast_fusion.1
  220.8 0.3 convolution_add_fusion
  221.2 5.8 %cholesky.128 = f32[64,64]{1,0:T(8,128)S(1)} custom-call(f32[64,64]{1,0:T(8,128)S(1)} %fusion.91), custom_call_target="Cholesky" | custom-call | tf_op jit(solution)/shard_map/jit(cholesky)/cholesky | solution.py:33
  227.0 0.6 compare_reduce_fusion
  227.7 0.7 fusion.86
  228.3 4.9 %custom-call.28 = f32[1,64,64]{1,2,0:T(8,128)S(1)} custom-call(f32[1,64,64]{2,1,0:T(8,128)S(1)} %fusion.86), custom_call_target="InvertDiagBlocksLowerTriangular" | custom-call | tf_op jit(solution)/shard_map/jit(_cho_solve)/triangular_solve | solution.py:35
  233.2 0.3 fusion.89
  233.9 0.7 maximum_bitcast_fusion
  234.5 0.6 maximum_bitcast_fusion.1
  (101 shorter events, 7.6 us)
Async XLA Ops:
  7.2 39.7 %all-gather.3.cloned.1.call-start = ((), (), s32[]{:S(2)}) async-start(), calls=%async_computation.1 | async-start | bytes 2621440 | tf_op jit(solution)/shard_map/all_gather | solution.py:82
  7.9 140.8 %reduce-scatter.2.cloned.1.call-start = ((), (), s32[]{:S(2)}) async-start(), calls=%async_computation.2 | async-start | bytes 2359296 | tf_op jit(solution)/shard_map/reduce_scatter | solution.py:118
  79.3 0.7 copy-start.1
  79.3 2.3 copy-start.3
  79.3 4.6 %copy-start.2 = (s32[2,64]{1,0:T(2,128)S(1)}, s32[2,64]{1,0:T(2,128)}, u32[]{:S(2)}) copy-start(s32[2,64]{1,0:T(2,128)} %param.20) | copy-start | bytes 1540
  82.4 4.0 %collective-permute-start.1 = (f32[16,64]{0,1:T(8,128)S(1)}, f32[16,64]{0,1:T(8,128)S(1)}, u32[]{:S(2)}, u32[]{:S(2)}) collective-permute-start(f32[16,64]{0,1:T(8,128)S(1)} %select_bitcast_fusion.3), channel_id=1, source_target_pairs={{0,1},{1,0},{2,3},{3,2},{4,5},{5,4},{6,7},{7,6},{8,9},{9,8},{10,11... | collective-permute-start | bytes 12296 | tf_op jit(solution)/shard_map/ppermute | solution.py:16
  87.2 5.5 %collective-permute-start.4 = (f32[16,64]{0,1:T(8,128)S(1)}, f32[16,64]{0,1:T(8,128)S(1)}, u32[]{:S(2)}, u32[]{:S(2)}) collective-permute-start(f32[16,64]{0,1:T(8,128)S(1)} %select_bitcast_fusion.2), channel_id=1, source_target_pairs={{0,2},{1,3},{2,0},{3,1},{4,6},{5,7},{6,4},{7,5},{8,10},{9,11},{10,... | collective-permute-start | bytes 12296 | tf_op jit(solution)/shard_map/ppermute | solution.py:16
  175.1 21.5 %copy-start = (f32[2,64,128]{2,1,0:T(8,128)}, f32[2,64,128]{2,1,0:T(8,128)S(1)}, u32[]{:S(2)}) copy-start(f32[2,64,128]{2,1,0:T(8,128)S(1)} %fusion.75) | copy-start | bytes 196612
  191.1 4.3 %collective-permute-start.2 = (f32[64,256]{1,0:T(8,128)S(1)}, f32[64,256]{1,0:T(8,128)S(1)}, u32[]{:S(2)}, u32[]{:S(2)}) collective-permute-start(f32[64,256]{1,0:T(8,128)S(1)} %fusion.64), channel_id=1, source_target_pairs={{0,1},{1,0},{2,3},{3,2},{4,5},{5,4},{6,7},{7,6},{8,9},{9,8},{10,11... | collective-permute-start | bytes 196616 | tf_op jit(solution)/shard_map/ppermute | solution.py:16
  192.1 4.3 %collective-permute-start = (f32[64,256]{1,0:T(8,128)S(1)}, f32[64,256]{1,0:T(8,128)S(1)}, u32[]{:S(2)}, u32[]{:S(2)}) collective-permute-start(f32[64,256]{1,0:T(8,128)S(1)} %get-tuple-element.110), channel_id=1, source_target_pairs={{0,1},{1,0},{2,3},{3,2},{4,5},{5,4},{6,7},{7,6},{8,9},{9,8},{10,11... | collective-permute-start | bytes 196616 | tf_op jit(solution)/shard_map/ppermute | solution.py:16
  211.9 4.3 %collective-permute-start.5 = (f32[64,256]{1,0:T(8,128)S(1)}, f32[64,256]{1,0:T(8,128)S(1)}, u32[]{:S(2)}, u32[]{:S(2)}) collective-permute-start(f32[64,256]{1,0:T(8,128)S(1)} %fusion.68), channel_id=1, source_target_pairs={{0,2},{1,3},{2,0},{3,1},{4,6},{5,7},{6,4},{7,5},{8,10},{9,11},{10,... | collective-permute-start | bytes 196616 | tf_op jit(solution)/shard_map/ppermute | solution.py:16
  213.9 4.3 %collective-permute-start.3 = (f32[64,256]{1,0:T(8,128)S(1)}, f32[64,256]{1,0:T(8,128)S(1)}, u32[]{:S(2)}, u32[]{:S(2)}) collective-permute-start(f32[64,256]{1,0:T(8,128)S(1)} %get-tuple-element.108), channel_id=1, source_target_pairs={{0,2},{1,3},{2,0},{3,1},{4,6},{5,7},{6,4},{7,5},{8,10},{9,11},{10,... | collective-permute-start | bytes 196616 | tf_op jit(solution)/shard_map/ppermute | solution.py:16
Sparse Core Ops, SparseCore 0:
  9.6 25.2 all-gather.2
  79.5 69.2 reduce-scatter.1
where the time goes:
time: 243 us; the launch traced here: 242 us
  waiting for transfers between devices  68.3 us (28%)
  other arithmetic  63.9 us (26%)
  blocking collectives  37.9 us (16%)
  matrix products  29.4 us (12%)
  between operations  16.6 us (7%)
  local copies, waits for them, and re-layouts  12.2 us (5%)
  loops' own time  7.83 us (3%)
  starting transfers between devices  5.96 us (2%)
    reduce_scatter x1, waiting for transfers between devices, local(): lax.psum_scatter(lax.map(one_block, starts).reshape(own_rows * lax.axis_s...  55.9 us
    another operation x13, other arithmetic, interpolate(): jnp.linalg.cholesky(gram_mat + damping * jnp.eye(chosen.shape[0], dtype=s...  31.4 us
    all_gather x1, blocking collectives, local(): row_coords = lax.all_gather(points[:, 0], 'col', axis=1, tiled=True)  31.2 us
    another operation x9, other arithmetic, interpolate(): solved = jax.scipy.linalg.cho_solve((factor, True), cross_mat.T)  26.7 us
    dot_general x4, matrix products, one_block(): return jnp.dot(kernel_tile, probe_cols, preferred_element_type=jnp.float32)  21.4 us
    ppermute x6, waiting for transfers between devices, swapped(): lax.ppermute(value, axis, [(i, i ^ 1 << bit) for i in range(lax.axis_size...  11.7 us
    another operation x1, loops' own time, local(): lax.map(one_block, starts).reshape(own_rows * lax.axis_size('col'), -1)  7.83 us
    all_gather x1, blocking collectives, local(): lax.all_gather(points, 'row', axis=2, tiled=True)  6.75 us
  transfers between devices with their start and end apart: 8, of which 7 were waited for; matrix products, arithmetic and copies ran while one was open for 3% of the time, Pallas kernels for 0%

commit v1 on v0

v1 whole, which is shorter than its diff:
```python
import math

import jax
import jax.numpy as jnp
import numpy as np
from jax import lax
from jax.experimental import pallas as pl
from jax.experimental.pallas import tpu as pltpu
from jax.sharding import PartitionSpec as P

LEAF = 128
FULL = lax.Precision.HIGHEST
F32 = jnp.float32
BF16 = jnp.bfloat16
DOUBLINGS = 9


def chebyshev_constants():
    taus = [1282.0 / 1280.0]
    for _ in range(DOUBLINGS):
        taus.append(2.0 * taus[-1] * taus[-1] - 1.0)
    front = 2.0**DOUBLINGS * math.prod(taus[:-1]) / taus[-1] / 640.0
    return taus[:-1], front


TAUS, FRONT = chebyshev_constants()


def split(value):
    high = value.astype(BF16).astype(F32)
    rest = value - high
    middle = rest.astype(BF16).astype(F32)
    return high, middle, rest - middle


def row_features(feats, gain):
    feats = feats.astype(F32)
    depth, width = feats.shape
    unit = math.log2(math.e) / (2.0 * depth)
    norm = jnp.sum(feats * feats, axis=0, keepdims=True) * -unit + math.log2(gain)
    parts = split(norm)
    place = lax.broadcasted_iota(jnp.int32, (16, width), 0)
    extra = jnp.where(place < 6, 1.0, 0.0)
    for pos in range(3):
        extra = jnp.where(place == pos, parts[pos], extra)
    return jnp.concatenate([*split(feats * (2.0 * unit)), extra], axis=0)


def col_features(feats):
    wide = feats.astype(F32)
    depth, width = wide.shape
    unit = math.log2(math.e) / (2.0 * depth)
    parts = split(jnp.sum(wide * wide, axis=0, keepdims=True) * -unit)
    place = lax.broadcasted_iota(jnp.int32, (16, width), 0)
    extra = jnp.where(place < 3, 1.0, 0.0)
    for pos in range(3):
        extra = jnp.where(place == pos + 3, parts[pos], extra)
    return jnp.concatenate([wide, wide, wide, extra], axis=0).astype(BF16)


def over(first, second, first_dim, second_dim, precision=None):
    return lax.dot_general(
        first,
        second,
        (((first_dim,), (second_dim,)), ((), ())),
        precision=precision,
        preferred_element_type=F32,
    )


def product_body(gain, span, first, last, chunk_count, source_count, *refs):
    refs = list(refs)
    sources = [refs.pop(0) for _ in range(source_count)]
    if first:
        row_points = [refs.pop(0) for _ in range(chunk_count)]
        rows_ref, acc_ref = refs
        for chunk in range(chunk_count):
            feats = row_points[chunk][...]
            rows_ref[pl.ds(chunk * span, span), :] = row_features(feats, gain).T.astype(BF16)
        acc_ref[...] = jnp.zeros_like(acc_ref)
    else:
        rows_ref, old_ref = refs[:2]
        if last:
            own_ref, *sent_refs, acc_ref = refs[2:]
        else:
            acc_ref = refs[2]
        acc_ref[...] = old_ref[...]

    def tile(source, quarter, diagonal):
        columns = col_features(source[quarter, pl.ds(span, 16), :])
        randoms = source[quarter, pl.ds(0, span), :]
        for chunk in range(chunk_count):
            rows = pl.ds(chunk * span, span)
            exponent = over(rows_ref[rows, :], columns, 1, 0)
            entries = jnp.exp2(exponent)
            if diagonal and chunk == 0:
                shape = (span, span)
                row_leaf = lax.broadcasted_iota(jnp.int32, shape, 0) // LEAF
                col_leaf = lax.broadcasted_iota(jnp.int32, shape, 1) // LEAF
                entries = jnp.where(row_leaf == col_leaf, 0.0, entries)
            acc_ref[rows, :] += over(entries.astype(BF16), randoms, 1, 0)

    for number, source in enumerate(sources):
        start = 0
        if first and number == 0:
            tile(source, 0, True)
            start = 1

        @pl.loop(start, source.shape[0])
        def _(quarter):
            tile(source, quarter, False)

    if last:
        own_ref[...] = acc_ref[pl.ds(0, span), :]
        for number, sent_ref in enumerate(sent_refs):
            sent_ref[...] = acc_ref[pl.ds((number + 1) * span, span), :].astype(BF16)


def product_cost(sources, rows, samples):
    columns = sum(s.shape[0] for s in sources) * (sources[0].shape[1] - 16)
    return pl.CostEstimate(
        flops=2 * rows * columns * (samples + 64),
        bytes_accessed=sum(2 * s.size for s in sources) + 8 * rows * samples,
        transcendentals=rows * columns,
    )


def product_start(sources, row_points, gain):
    span = sources[0].shape[1] - 16
    samples = sources[0].shape[2]
    chunks = len(row_points)
    rows = chunks * span
    return pl.pallas_call(
        lambda *refs: product_body(gain, span, True, False, chunks, len(sources), *refs),
        out_shape=(
            jax.ShapeDtypeStruct((rows, 64), BF16),
            jax.ShapeDtypeStruct((rows, samples), F32),
        ),
        cost_estimate=product_cost(sources, rows, samples),
        compiler_params=pltpu.CompilerParams(vmem_limit_bytes=48 << 20),
        name="product_start",
    )(*sources, *row_points)


def product_next(sources, row_feats, total, last):
    span = sources[0].shape[1] - 16
    rows, samples = total.shape
    chunks = rows // span
    if last:
        out_shape = [jax.ShapeDtypeStruct((span, samples), F32)]
        out_shape += [jax.ShapeDtypeStruct((span, samples), BF16)] * (chunks - 1)
        scratch = [pltpu.VMEM((rows, samples), F32)]
    else:
        out_shape = jax.ShapeDtypeStruct((rows, samples), F32)
        scratch = []
    return pl.pallas_call(
        lambda *refs: product_body(0.0, span, False, last, chunks, len(sources), *refs),
        out_shape=out_shape,
        scratch_shapes=scratch,
        cost_estimate=product_cost(sources, rows, samples),
        compiler_params=pltpu.CompilerParams(vmem_limit_bytes=48 << 20),
        name="product_last" if last else "product_next",
    )(*sources, row_feats, total)


def one_hot(chosen, pool):
    place = lax.broadcasted_iota(jnp.int32, (pool, chosen.shape[1]), 0)
    return jnp.where(place == chosen, 1.0, 0.0).astype(F32)


def interpolate(stacked, picks):
    rank = picks.shape[1]
    skeleton = over(picks, stacked, 0, 0, FULL)
    cross = over(skeleton, stacked, 1, 1, FULL)
    gram = over(skeleton, skeleton, 1, 1, FULL)
    ridge = 0.05 * jnp.sum(skeleton * skeleton, keepdims=True) / rank + 1e-05
    eye = jnp.where(
        lax.broadcasted_iota(jnp.int32, (rank, rank), 0)
        == lax.broadcasted_iota(jnp.int32, (rank, rank), 1),
        1.0,
        0.0,
    )
    inverse = 1.0 / (640.0 * ridge)
    power = eye - gram * inverse
    solved = cross
    pool = cross.shape[1]
    for number, tau in enumerate(TAUS):
        if number < DOUBLINGS - 1:
            both = over(power, jnp.concatenate([solved, power], axis=1), 1, 0, FULL)
            solved = solved + both[:, :pool] * (1.0 / tau)
            power = 2.0 * both[:, pool:] - eye
        else:
            solved = solved + over(power, solved, 1, 0, FULL) * (1.0 / tau)
    return solved * (inverse * (FRONT * 640.0)), skeleton


def merge(first, second, picks, gain):
    first_samples, first_reduced, first_points = first
    second_samples, second_reduced, second_points = second
    rank = first_samples.shape[0]
    upper = jnp.exp2(
        over(row_features(first_points, gain).astype(BF16), col_features(second_points), 0, 0)
    )
    lower = jnp.exp2(
        over(row_features(second_points, gain).astype(BF16), col_features(first_points), 0, 0)
    )
    stacked = jnp.concatenate(
        [
            first_samples - over(upper, second_reduced, 1, 0, FULL),
            second_samples - over(lower, first_reduced, 1, 0, FULL),
        ],
        axis=0,
    )
    interp, skeleton = interpolate(stacked, picks)
    reduced = over(interp, jnp.concatenate([first_reduced, second_reduced], axis=0), 1, 0, FULL)
    points = over(first_points, picks[:rank], 1, 0) + over(second_points, picks[rank:], 1, 0)
    return interp, (skeleton, reduced, points)


def store_state(state_ref, state):
    samples, reduced, points = state
    rank = samples.shape[0]
    state_ref[pl.ds(0, rank), :] = samples
    state_ref[pl.ds(rank, rank), :] = reduced
    state_ref[pl.ds(2 * rank, points.shape[0]), :] = jnp.concatenate(
        [points] * (state_ref.shape[1] // rank), axis=1
    )


def load_state(state, rank):
    return (state[:rank], state[rank : 2 * rank], state[2 * rank :, :rank])


def leaves_body(gain, received, *refs):
    own_ref, *others = refs[: received + 1]
    source_ref, leaf_skeleton_ref, skeleton_ref, leaf_ref, upper_ref, state_ref = refs[received + 1 :]
    span = own_ref.shape[0]
    total = own_ref[...]
    for other in others:
        total = total + other[...].astype(F32)
    children = []
    for leaf in range(span // LEAF):
        rows = slice(leaf * LEAF, (leaf + 1) * LEAF)
        picks = one_hot(leaf_skeleton_ref[leaf : leaf + 1, :], LEAF)
        interp, skeleton = interpolate(total[rows], picks)
        leaf_ref[leaf] = interp.T
        randoms = source_ref[0, pl.ds(leaf * LEAF, LEAF), :].astype(F32)
        feats = source_ref[0, pl.ds(span, 16), pl.ds(leaf * LEAF, LEAF)].astype(F32)
        children.append(
            (skeleton, over(interp, randoms, 1, 0, FULL), over(feats, picks, 1, 0))
        )
    interp, state = merge(*children, one_hot(skeleton_ref[...], LEAF), gain)
    upper_ref[...] = interp.T
    store_state(state_ref, state)


def leaves(own, others, source, leaf_skeleton, skeleton, gain):
    span, samples = own.shape
    leaf_count, rank = leaf_skeleton.shape
    return pl.pallas_call(
        lambda *refs: leaves_body(gain, len(others), *refs),
        out_shape=(
            jax.ShapeDtypeStruct((leaf_count, LEAF, rank), F32),
            jax.ShapeDtypeStruct((2 * rank, rank), F32),
            jax.ShapeDtypeStruct((2 * rank + 16, samples), F32),
        ),
        cost_estimate=pl.CostEstimate(flops=10**9, bytes_accessed=10**6, transcendentals=10**4),
        compiler_params=pltpu.CompilerParams(vmem_limit_bytes=48 << 20),
        name="leaves",
    )(own, *others, source, leaf_skeleton, skeleton)


def level_body(gain, place_ref, mine_ref, theirs_ref, table_ref, *refs):
    rank = table_ref.shape[1]
    mine_first = place_ref[0] == 0
    mine, theirs = mine_ref[...], theirs_ref[...]
    first = load_state(jnp.where(mine_first, mine, theirs), rank)
    second = load_state(jnp.where(mine_first, theirs, mine), rank)
    picks = one_hot(table_ref[pl.ds(place_ref[1], 1), :], 2 * rank)
    interp, state = merge(first, second, picks, gain)
    if len(refs) == 2:
        upper_ref, state_ref = refs
        upper_ref[...] = interp.T
        store_state(state_ref, state)
    else:
        one_ref, two_ref, upper_ref, top_ref = refs
        upper_ref[0, 0] = one_ref[...]
        upper_ref[1, 0] = two_ref[...]
        upper_ref[2, 0] = interp.T
        top_ref[0, 0] = state[0]
        top_ref[1, 0] = state[1]


def level(place, mine, theirs, table, gain, below=()):
    rank = table.shape[1]
    if below:
        out_shape = (
            jax.ShapeDtypeStruct((3, 1, 2 * rank, rank), F32),
            jax.ShapeDtypeStruct((2, 1, rank, mine.shape[1]), F32),
        )
    else:
        out_shape = (
            jax.ShapeDtypeStruct((2 * rank, rank), F32),
            jax.ShapeDtypeStruct(mine.shape, F32),
        )
    vmem = pl.BlockSpec(memory_space=pltpu.VMEM)
    return pl.pallas_call(
        lambda *refs: level_body(gain, *refs),
        out_shape=out_shape,
        in_specs=[pl.BlockSpec(memory_space=pltpu.SMEM)] + [vmem] * (3 + len(below)),
        cost_estimate=pl.CostEstimate(flops=10**9, bytes_accessed=10**6, transcendentals=10**4),
        compiler_params=pltpu.CompilerParams(vmem_limit_bytes=48 << 20),
        name="level",
    )(place, mine, theirs, table, *below)


def local(probes, points, leaf_skeleton, skeleton_one, skeleton_two, skeleton_three):
    own_rows = probes.shape[1]
    row_count = lax.axis_size("row")
    col_count = lax.axis_size("col")
    col_pos = lax.axis_index("col")
    gain = 16.0 / math.sqrt(4 * own_rows * row_count * col_count)

    def swap(value, row_bits, col_bits):
        pairs = [
            (r * col_count + c, (r ^ row_bits) * col_count + (c ^ col_bits))
            for r in range(row_count)
            for c in range(col_count)
        ]
        return lax.ppermute(value, ("row", "col"), pairs)

    own = jnp.concatenate([probes, points.transpose(1, 0, 2)], axis=1)
    half = own.shape[0] // 2
    own_points = points[:, 0]
    row_points = [own_points]
    for offset in range(1, col_count // 2):
        row_points.append(swap(own_points, 0, 2 * offset))
    sibling = swap(own, 1, 0)
    beside = swap(own, 0, 1)
    across = swap(own, 2, 0)
    beside_sibling = swap(beside, 1, 0)
    across_sibling = swap(across, 1, 0)
    diagonal = [swap(beside[:half], 2, 0), swap(across[half:], 0, 1)]
    diagonal_sibling = [swap(value, 1, 0) for value in diagonal]
    groups = [[beside, across], [beside_sibling, across_sibling], diagonal, diagonal_sibling]
    for bit in range(2, row_count.bit_length() - 1):
        everything = [own, sibling] + [value for group in groups for value in group]
        groups.append([swap(value, 1 << bit, 0) for value in everything])
    row_feats, total = product_start([own, sibling], row_points, gain)
    for number, group in enumerate(groups):
        total = product_next(group, row_feats, total, number == len(groups) - 1)
    kept, *sent = total
    received = [swap(value, 0, 2 * (number + 1)) for number, value in enumerate(sent)]

    leaf_interp, interp_one, state = leaves(
        kept, received, own, leaf_skeleton, skeleton_one, gain
    )
    place = jnp.stack([col_pos & 1, col_pos >> 1]).astype(jnp.int32)
    interp_two, state_two = level(place, state, swap(state, 0, 1), skeleton_two, gain)
    place = jnp.stack([col_pos >> 1 & 1, col_pos >> 2]).astype(jnp.int32)
    upper_interp, top_state = level(
        place,
        state_two,
        swap(state_two, 0, 2),
        skeleton_three,
        gain,
        (interp_one, interp_two),
    )
    return leaf_interp, upper_interp, top_state


def solution(mesh):
    placed = (
        P(None, ("row", "col"), None),
        P(None, None, ("row", "col")),
        P(("row", "col"), None),
        P(("row", "col"), None),
        P("row", None),
        P("row", None),
    )
    return jax.shard_map(
        local,
        mesh=mesh,
        in_specs=placed,
        out_specs=(
            P(("row", "col"), None, None),
            P(None, ("row", "col"), None, None),
            P(None, ("row", "col"), None, None),
        ),
        check_vma=False,
    )
```

time: 243 us -> 93.5 us (0.38)
  other arithmetic: 63.9 us -> 1.23 us
  waiting for transfers between devices: 68.3 us -> 30 us
  blocking collectives: 37.9 us -> 0 us
  Pallas kernels: 0 us -> 36 us
  matrix products: 29.4 us -> 0 us
  starting transfers between devices: 5.96 us -> 22.9 us
  between operations: 16.6 us -> 0.8 us
  local copies, waits for them, and re-layouts: 12.2 us -> 2.3 us
  loops' own time: 7.83 us -> 0 us
    another operation x23 -> x2, other arithmetic: 58.9 us -> 0.15 us  [the longest x1 0.07 us: local(): place = jnp.stack([col_pos & 1, col_pos >> 1]).astype(jnp.int32)]
    reduce_scatter x1 -> x0, waiting for transfers between devices: 55.9 us -> none  [local(): lax.psum_scatter(lax.map(one_block, starts).reshape(own_rows * lax.axis_s...]
    all_gather x2 -> x0, blocking collectives: 37.9 us -> none  [the longest x1 31.2 us: local(): row_coords = lax.all_gather(points[:, 0], 'col', axis=1, tiled=True)]
    pallas_call x0 -> x8, Pallas kernels: none -> 36 us  [the longest x4 15.1 us: product_next(): pl.pallas_call(lambda *refs: product_body(0.0, span, False, last, chunks,...]
    dot_general x28 -> x0, matrix products: 27.7 us -> none  [the longest x4 21.4 us: one_block(): return jnp.dot(kernel_tile, probe_cols, preferred_element_type=jnp.float32)]
    ppermute x6 -> x17, waiting for transfers between devices: 11.7 us -> 30 us  [swap(): return lax.ppermute(value, ('row', 'col'), pairs)]
    ppermute x6 -> x17, starting transfers between devices: 5.89 us -> 22.9 us  [swap(): return lax.ppermute(value, ('row', 'col'), pairs)]
    another operation x1 -> x0, loops' own time: 7.83 us -> none  [local(): lax.map(one_block, starts).reshape(own_rows * lax.axis_size('col'), -1)]
  transfers between devices with their start and end apart: 8 -> 17, of which waited for: 7 -> 8; matrix products, arithmetic and copies ran while one was open for 3% -> 1% of each run, Pallas kernels for 0% -> 19%
where the time goes in v1:
time: 93.5 us; the launch traced here: 93.3 us
  Pallas kernels  36 us (39%)
  waiting for transfers between devices  30 us (32%)
  starting transfers between devices  22.9 us (24%)
  local copies, waits for them, and re-layouts  2.3 us (2%)
  other arithmetic  1.23 us (1%)
    ppermute x17, waiting for transfers between devices, swap(): return lax.ppermute(value, ('row', 'col'), pairs)  30 us
    ppermute x17, starting transfers between devices, swap(): return lax.ppermute(value, ('row', 'col'), pairs)  22.9 us
    pallas_call x4, Pallas kernels, product_next(): pl.pallas_call(lambda *refs: product_body(0.0, span, False, last, chunks,...  15.1 us
    pallas_call x2, Pallas kernels, level(): pl.pallas_call(lambda *refs: level_body(gain, *refs), out_shape=out_shape...  7.98 us
    pallas_call x1, Pallas kernels, leaves(): pl.pallas_call(lambda *refs: leaves_body(gain, len(others), *refs), out_s...  7.96 us
    pallas_call x1, Pallas kernels, product_start(): pl.pallas_call(lambda *refs: product_body(gain, span, True, False, chunks...  4.95 us
    unnamed x11, local copies, waits for them, and re-layouts  2.26 us
  transfers between devices with their start and end apart: 17, of which 8 were waited for; matrix products, arithmetic and copies ran while one was open for 1% of the time, Pallas kernels for 19%

profile of v1, /device:TPU:0, one launch (start us, length us, event | category | flops | bytes accessed | tf_op | source)
XLA Modules:
  0.0 93.3 jit_solution(5117808170302435443)
XLA Ops:
  0.6 0.8 copy.15
  1.4 1.1 %pad_maximum_fusion.refs_0_.refs_4_ = bf16[4,272,256]{2,1,0:T(8,128)(2,1)S(1)} fusion(bf16[4,16,256]{2,1,0:T(8,128)(2,1)S(1)} %bitcast.8, bf16[4,256,256]{2,1,0:T(8,128)(2,1)} %param.6), kind=kLoop, calls=%fused_computation | loop fusion | flops 1114112 | bytes 1114112 | tf_op jit(solution)/shard_map/concatenate | solution.py:332
  2.5 3.0 %collective-permute-start = (bf16[4,272,256]{2,1,0:T(8,128)(2,1)S(1)}, bf16[4,272,256]{2,1,0:T(8,128)(2,1)S(1)}, u32[]{:S(2)}, u32[]{:S(2)}) collective-permute-start(bf16[4,272,256]{2,1,0:T(8,128)(2,1)S(1)} %pad_maximum_fusion.refs_0_.refs_4_), channel_id=1, source_target_pairs={{0,1},{1,0},{2,3},{3,2},{4,5},{5,4},{6,7},{7,6},{8,9},{9,8},{10,11... | collective-permute-start | bytes 1671176 | tf_op jit(solution)/shard_map/ppermute | solution.py:330
  5.5 1.5 %collective-permute-start.3 = (bf16[4,272,256]{2,1,0:T(8,128)(2,1)S(1)}, bf16[4,272,256]{2,1,0:T(8,128)(2,1)S(1)}, u32[]{:S(2)}, u32[]{:S(2)}) collective-permute-start(bf16[4,272,256]{2,1,0:T(8,128)(2,1)S(1)} %pad_maximum_fusion.refs_0_.refs_4_), channel_id=1, source_target_pairs={{0,16},{1,17},{2,18},{3,19},{4,20},{5,21},{6,22},{7,23},{8,24},{9,... | collective-permute-start | bytes 1671176 | tf_op jit(solution)/shard_map/ppermute | solution.py:330
  7.0 0.0 collective-permute-start.6
  7.0 11.1 %collective-permute-done.refs_0_ = bf16[4,272,256]{2,1,0:T(8,128)(2,1)S(1)} collective-permute-done((bf16[4,272,256]{2,1,0:T(8,128)(2,1)S(1)}, bf16[4,272,256]{2,1,0:T(8,128)(2,1)S(1)}, u32[]{:S(2)}, u32[]{:S(2)}) %collective-permute-start) | collective-permute-done | bytes 557088 | tf_op jit(solution)/shard_map/ppermute | solution.py:330
  18.1 0.0 collective-permute-start.10
  18.1 1.5 %collective-permute-done.3.refs_1_ = bf16[4,272,256]{2,1,0:T(8,128)(2,1)S(1)} collective-permute-done((bf16[4,272,256]{2,1,0:T(8,128)(2,1)S(1)}, bf16[4,272,256]{2,1,0:T(8,128)(2,1)S(1)}, u32[]{:S(2)}, u32[]{:S(2)}) %collective-permute-start.3) | collective-permute-done | bytes 557088 | tf_op jit(solution)/shard_map/ppermute | solution.py:330
  19.6 0.0 collective-permute-start.11
  19.6 1.6 %collective-permute-start.7 = (bf16[16,256]{1,0:T(8,128)(2,1)S(1)}, bf16[16,256]{1,0:T(8,128)(2,1)S(1)}, u32[]{:S(2)}, u32[]{:S(2)}) collective-permute-start(bf16[16,256]{1,0:T(8,128)(2,1)S(1)} %slice_bitcast_fusion.refs_2_), channel_id=1, source_target_pairs={{0,2},{1,3},{2,0},{3,1},{4,6},{5,7},{6,4},{7,5},{8,10},{9,11},{10,... | collective-permute-start | bytes 24584 | tf_op jit(solution)/shard_map/ppermute | solution.py:330
  21.1 2.6 %collective-permute-start.8 = (bf16[16,256]{1,0:T(8,128)(2,1)S(1)}, bf16[16,256]{1,0:T(8,128)(2,1)S(1)}, u32[]{:S(2)}, u32[]{:S(2)}) collective-permute-start(bf16[16,256]{1,0:T(8,128)(2,1)S(1)} %slice_bitcast_fusion.refs_2_), channel_id=1, source_target_pairs={{0,4},{1,5},{2,6},{3,7},{4,0},{5,1},{6,2},{7,3},{8,12},{9,13},{10,... | collective-permute-start | bytes 24584 | tf_op jit(solution)/shard_map/ppermute | solution.py:330
  23.7 0.0 collective-permute-done.7.refs_3_
  23.7 3.1 %collective-permute-start.9 = (bf16[16,256]{1,0:T(8,128)(2,1)S(1)}, bf16[16,256]{1,0:T(8,128)(2,1)S(1)}, u32[]{:S(2)}, u32[]{:S(2)}) collective-permute-start(bf16[16,256]{1,0:T(8,128)(2,1)S(1)} %slice_bitcast_fusion.refs_2_), channel_id=1, source_target_pairs={{0,6},{1,7},{2,4},{3,5},{4,2},{5,3},{6,0},{7,1},{8,14},{9,15},{10,... | collective-permute-start | bytes 24584 | tf_op jit(solution)/shard_map/ppermute | solution.py:330
  26.9 0.0 collective-permute-done.8.refs_4_
  26.9 1.6 %collective-permute-start.1 = (bf16[2,272,256]{2,1,0:T(8,128)(2,1)S(1)}, bf16[2,272,256]{2,1,0:T(8,128)(2,1)S(1)}, u32[]{:S(2)}, u32[]{:S(2)}) collective-permute-start(bf16[2,272,256]{2,1,0:T(8,128)(2,1)S(1)} %slice.12), channel_id=1, source_target_pairs={{0,16},{1,17},{2,18},{3,19},{4,20},{5,21},{6,22},{7,23},{8,24},{9,... | collective-permute-start | bytes 835592 | tf_op jit(solution)/shard_map/ppermute | solution.py:330
  28.5 0.7 collective-permute-done.9.refs_5_
  29.2 0.8 collective-permute-start.4
  30.0 0.0 collective-permute-done.6.refs_1_
  30.0 5.0 %product_start.1 = (bf16[1024,64]{1,0:T(8,128)(2,1)S(1)}, f32[1024,256]{1,0:T(8,128)S(1)}) custom-call(bf16[4,272,256]{2,1,0:T(8,128)(2,1)S(1)} %pad_maximum_fusion.refs_0_.refs_4_, bf16[4,272,256]{2,1,0:T(8,128)(2,1)S(1)} %collective-permute-done.6.refs_1_, bf16[16,256]{1,0:T(8,128)(2,1)S(1)} %slice_bitcast_fusion.refs_2_, ...), custom_call_target="tpu_custom_call" | custom-call | flops 1342177280 | bytes 3211264 | tf_op jit(solution)/shard_map/product_start/pallas_call | solution.py:133
  34.9 0.0 collective-permute-done.1.refs_0_
  35.0 0.1 collective-permute-start.2
  35.0 1.5 %collective-permute-done.4.refs_1_ = bf16[2,272,256]{2,1,0:T(8,128)(2,1)S(1)} collective-permute-done((bf16[2,272,256]{2,1,0:T(8,128)(2,1)S(1)}, bf16[2,272,256]{2,1,0:T(8,128)(2,1)S(1)}, u32[]{:S(2)}, u32[]{:S(2)}) %collective-permute-start.4) | collective-permute-done | bytes 278560 | tf_op jit(solution)/shard_map/ppermute | solution.py:330
  36.6 0.0 collective-permute-start.5
  36.6 4.9 %product_next.3.refs_3_ = f32[1024,256]{1,0:T(8,128)S(1)} custom-call(bf16[4,272,256]{2,1,0:T(8,128)(2,1)S(1)} %collective-permute-done.refs_0_, bf16[4,272,256]{2,1,0:T(8,128)(2,1)S(1)} %collective-permute-done.3.refs_1_, bf16[1024,64]{1,0:T(8,128)(2,1)S(1)} %get-tuple-element.16.refs_2_, f32[1024,256]{1,0:T(8,128)S(1)} %get-tuple-element.17.refs_3_), custom_call_target="tpu_custom_call" | custom-call | flops 1342177280 | bytes 3211264 | tf_op jit(solution)/shard_map/product_next/pallas_call | solution.py:156
  41.5 0.0 collective-permute-done.10.refs_0_
  41.5 0.0 collective-permute-done.11.refs_1_
  41.5 4.9 %product_next.4.refs_3_ = f32[1024,256]{1,0:T(8,128)S(1)} custom-call(bf16[4,272,256]{2,1,0:T(8,128)(2,1)S(1)} %collective-permute-done.10.refs_0_, bf16[4,272,256]{2,1,0:T(8,128)(2,1)S(1)} %collective-permute-done.11.refs_1_, bf16[1024,64]{1,0:T(8,128)(2,1)S(1)} %get-tuple-element.16.refs_2_, f32[1024,256]{1,0:T(8,128)S(1)} %product_next.3.refs_3_), custom_call_target="tpu_custom_call" | custom-call | flops 1342177280 | bytes 3211264 | tf_op jit(solution)/shard_map/product_next/pallas_call | solution.py:156
  46.5 2.5 %product_next.5.refs_3_ = f32[1024,256]{1,0:T(8,128)S(1)} custom-call(bf16[2,272,256]{2,1,0:T(8,128)(2,1)S(1)} %collective-permute-done.1.refs_0_, bf16[2,272,256]{2,1,0:T(8,128)(2,1)S(1)} %collective-permute-done.4.refs_1_, bf16[1024,64]{1,0:T(8,128)(2,1)S(1)} %get-tuple-element.16.refs_2_, f32[1024,256]{1,0:T(8,128)S(1)} %product_next.4.refs_3_), custom_call_target="tpu_custom_call" | custom-call | flops 671088640 | bytes 2654208 | tf_op jit(solution)/shard_map/product_next/pallas_call | solution.py:156
  49.0 0.0 copy-start.1
  49.0 0.0 copy-start.3
  49.0 0.0 collective-permute-done.2.refs_0_
  49.0 0.0 collective-permute-done.5.refs_1_
  49.0 2.7 %product_last.1 = (f32[256,256]{1,0:T(8,128)S(1)}, bf16[256,256]{1,0:T(8,128)(2,1)S(1)}, bf16[256,256]{1,0:T(8,128)(2,1)S(1)}, bf16[256,256]{1,0:T(8,128)(2,1)S(1)}) custom-call(bf16[2,272,256]{2,1,0:T(8,128)(2,1)S(1)} %collective-permute-done.2.refs_0_, bf16[2,272,256]{2,1,0:T(8,128)(2,1)S(1)} %collective-permute-done.5.refs_1_, ...), custom_call_target="tpu_custom_call" | custom-call | flops 671088640 | bytes 2654208 | tf_op jit(solution)/shard_map/product_last/pallas_call | solution.py:156
  51.8 0.1 collective-permute-start.12
  51.8 3.1 %collective-permute-start.13 = (bf16[256,256]{1,0:T(8,128)(2,1)S(1)}, bf16[256,256]{1,0:T(8,128)(2,1)S(1)}, u32[]{:S(2)}, u32[]{:S(2)}) collective-permute-start(bf16[256,256]{1,0:T(8,128)(2,1)S(1)} %get-tuple-element.20), channel_id=1, source_target_pairs={{0,4},{1,5},{2,6},{3,7},{4,0},{5,1},{6,2},{7,3},{8,12},{9,13},{10,... | collective-permute-start | bytes 393224 | tf_op jit(solution)/shard_map/ppermute | solution.py:330
  54.9 1.3 %collective-permute-start.14 = (bf16[256,256]{1,0:T(8,128)(2,1)S(1)}, bf16[256,256]{1,0:T(8,128)(2,1)S(1)}, u32[]{:S(2)}, u32[]{:S(2)}) collective-permute-start(bf16[256,256]{1,0:T(8,128)(2,1)S(1)} %get-tuple-element.21), channel_id=1, source_target_pairs={{0,6},{1,7},{2,4},{3,5},{4,2},{5,3},{6,0},{7,1},{8,14},{9,15},{10,... | collective-permute-start | bytes 393224 | tf_op jit(solution)/shard_map/ppermute | solution.py:330
  56.2 4.0 %collective-permute-done.12.refs_1_ = bf16[256,256]{1,0:T(8,128)(2,1)S(1)} collective-permute-done((bf16[256,256]{1,0:T(8,128)(2,1)S(1)}, bf16[256,256]{1,0:T(8,128)(2,1)S(1)}, u32[]{:S(2)}, u32[]{:S(2)}) %collective-permute-start.12) | collective-permute-done | bytes 131104 | tf_op jit(solution)/shard_map/ppermute | solution.py:330
  60.2 4.6 %collective-permute-done.13.refs_2_ = bf16[256,256]{1,0:T(8,128)(2,1)S(1)} collective-permute-done((bf16[256,256]{1,0:T(8,128)(2,1)S(1)}, bf16[256,256]{1,0:T(8,128)(2,1)S(1)}, u32[]{:S(2)}, u32[]{:S(2)}) %collective-permute-start.13) | collective-permute-done | bytes 131104 | tf_op jit(solution)/shard_map/ppermute | solution.py:330
  64.8 0.0 collective-permute-done.14.refs_3_
  64.8 0.0 copy-done.1
  64.8 0.0 copy-done.3
  64.8 0.0 copy-start
  64.9 8.0 %leaves.1 = (f32[2,128,64]{2,1,0:T(8,128)S(1)}, f32[128,64]{1,0:T(8,128)S(1)}, f32[144,256]{1,0:T(8,128)S(1)}) custom-call(f32[256,256]{1,0:T(8,128)S(1)} %get-tuple-element.18.refs_0_, bf16[256,256]{1,0:T(8,128)(2,1)S(1)} %collective-permute-done.12.refs_1_, bf16[256,256]{1,0:T(8,128)(2,1)S(1)} %collective-permute-done.13.refs_2_, ...), custom_call_target="tpu_custom_call" | custom-call | flops 1000000000 | bytes 1000000 | tf_op jit(solution)/shard_map/leaves/pallas_call | solution.py:260
  72.8 0.9 collective-permute-start.15
  73.7 0.1 pad_add_fusion.1.refs_0_
  73.8 0.0 copy-start.2
  73.8 4.2 %collective-permute-done.15.refs_2_ = f32[144,256]{1,0:T(8,128)S(1)} collective-permute-done((f32[144,256]{1,0:T(8,128)S(1)}, f32[144,256]{1,0:T(8,128)S(1)}, u32[]{:S(2)}, u32[]{:S(2)}) %collective-permute-start.15) | collective-permute-done | bytes 147488 | tf_op jit(solution)/shard_map/ppermute | solution.py:330
  78.0 0.0 copy-done
  78.0 3.7 %level.2 = (f32[128,64]{1,0:T(8,128)S(1)}, f32[144,256]{1,0:T(8,128)S(1)}) custom-call(s32[2]{0:T(128)S(1)} %pad_add_fusion.1.refs_0_, f32[144,256]{1,0:T(8,128)S(1)} %get-tuple-element.23.refs_1_, f32[144,256]{1,0:T(8,128)S(1)} %collective-permute-done.15.refs_2_, s32[4,64]{1,0:T(4,128)S(1)} %copy-done), custom_call_target="tpu_custom_call" | custom-call | flops 1000000000 | bytes 1000000 | tf_op jit(solution)/shard_map/level/pallas_call | solution.py:307
  81.7 3.4 %collective-permute-start.16 = (f32[144,256]{1,0:T(8,128)S(1)}, f32[144,256]{1,0:T(8,128)S(1)}, u32[]{:S(2)}, u32[]{:S(2)}) collective-permute-start(f32[144,256]{1,0:T(8,128)S(1)} %get-tuple-element.24.refs_1_), channel_id=1, source_target_pairs={{0,2},{1,3},{2,0},{3,1},{4,6},{5,7},{6,4},{7,5},{8,10},{9,11},{10,... | collective-permute-start | bytes 442376 | tf_op jit(solution)/shard_map/ppermute | solution.py:330
  85.1 0.1 pad_add_fusion.refs_0_
  85.2 0.7 copy.11
  85.9 2.3 %collective-permute-done.16.refs_2_ = f32[144,256]{1,0:T(8,128)S(1)} collective-permute-done((f32[144,256]{1,0:T(8,128)S(1)}, f32[144,256]{1,0:T(8,128)S(1)}, u32[]{:S(2)}, u32[]{:S(2)}) %collective-permute-start.16) | collective-permute-done | bytes 147488 | tf_op jit(solution)/shard_map/ppermute | solution.py:330
  88.2 0.0 copy-done.2
  88.2 4.3 %level.3 = (f32[3,1,128,64]{3,2,1,0:T(8,128)S(1)}, f32[2,1,64,256]{3,2,1,0:T(8,128)}) custom-call(s32[2]{0:T(128)S(1)} %pad_add_fusion.refs_0_, f32[144,256]{1,0:T(8,128)S(1)} %get-tuple-element.24.refs_1_, f32[144,256]{1,0:T(8,128)S(1)} %collective-permute-done.16.refs_2_, s32[2,64]{1,0:T(2,128)S(1)} %copy-done.2, f32[128,64]{1,0:T(8,128)S(1)} %get-tuple-element.25.refs_4_, ...), custom_call_target="tpu_custom_call" | custom-call | flops 1000000000 | bytes 1000000 | tf_op jit(solution)/shard_map/level/pallas_call | solution.py:307
  92.5 0.8 copy.12
  (3 shorter events, 0.0 us)
Async XLA Ops:
  2.5 15.6 %collective-permute-start = (bf16[4,272,256]{2,1,0:T(8,128)(2,1)S(1)}, bf16[4,272,256]{2,1,0:T(8,128)(2,1)S(1)}, u32[]{:S(2)}, u32[]{:S(2)}) collective-permute-start(bf16[4,272,256]{2,1,0:T(8,128)(2,1)S(1)} %pad_maximum_fusion.refs_0_.refs_4_), channel_id=1, source_target_pairs={{0,1},{1,0},{2,3},{3,2},{4,5},{5,4},{6,7},{7,6},{8,9},{9,8},{10,11... | collective-permute-start | bytes 1671176 | tf_op jit(solution)/shard_map/ppermute | solution.py:330
  5.5 14.1 %collective-permute-start.3 = (bf16[4,272,256]{2,1,0:T(8,128)(2,1)S(1)}, bf16[4,272,256]{2,1,0:T(8,128)(2,1)S(1)}, u32[]{:S(2)}, u32[]{:S(2)}) collective-permute-start(bf16[4,272,256]{2,1,0:T(8,128)(2,1)S(1)} %pad_maximum_fusion.refs_0_.refs_4_), channel_id=1, source_target_pairs={{0,16},{1,17},{2,18},{3,19},{4,20},{5,21},{6,22},{7,23},{8,24},{9,... | collective-permute-start | bytes 1671176 | tf_op jit(solution)/shard_map/ppermute | solution.py:330
  7.0 23.0 %collective-permute-start.6 = (bf16[4,272,256]{2,1,0:T(8,128)(2,1)S(1)}, bf16[4,272,256]{2,1,0:T(8,128)(2,1)S(1)}, u32[]{:S(2)}, u32[]{:S(2)}) collective-permute-start(bf16[4,272,256]{2,1,0:T(8,128)(2,1)S(1)} %pad_maximum_fusion.refs_0_.refs_4_), channel_id=1, source_target_pairs={{0,8},{1,9},{2,10},{3,11},{4,12},{5,13},{6,14},{7,15},{8,0},{9,1},... | collective-permute-start | bytes 1671176 | tf_op jit(solution)/shard_map/ppermute | solution.py:330
  18.1 23.4 %collective-permute-start.10 = (bf16[4,272,256]{2,1,0:T(8,128)(2,1)S(1)}, bf16[4,272,256]{2,1,0:T(8,128)(2,1)S(1)}, u32[]{:S(2)}, u32[]{:S(2)}) collective-permute-start(bf16[4,272,256]{2,1,0:T(8,128)(2,1)S(1)} %collective-permute-done.refs_0_), channel_id=1, source_target_pairs={{0,8},{1,9},{2,10},{3,11},{4,12},{5,13},{6,14},{7,15},{8,0},{9,1},... | collective-permute-start | bytes 1671176 | tf_op jit(solution)/shard_map/ppermute | solution.py:330
  19.6 22.0 %collective-permute-start.11 = (bf16[4,272,256]{2,1,0:T(8,128)(2,1)S(1)}, bf16[4,272,256]{2,1,0:T(8,128)(2,1)S(1)}, u32[]{:S(2)}, u32[]{:S(2)}) collective-permute-start(bf16[4,272,256]{2,1,0:T(8,128)(2,1)S(1)} %collective-permute-done.3.refs_1_), channel_id=1, source_target_pairs={{0,8},{1,9},{2,10},{3,11},{4,12},{5,13},{6,14},{7,15},{8,0},{9,1},... | collective-permute-start | bytes 1671176 | tf_op jit(solution)/shard_map/ppermute | solution.py:330
  19.6 4.2 %collective-permute-start.7 = (bf16[16,256]{1,0:T(8,128)(2,1)S(1)}, bf16[16,256]{1,0:T(8,128)(2,1)S(1)}, u32[]{:S(2)}, u32[]{:S(2)}) collective-permute-start(bf16[16,256]{1,0:T(8,128)(2,1)S(1)} %slice_bitcast_fusion.refs_2_), channel_id=1, source_target_pairs={{0,2},{1,3},{2,0},{3,1},{4,6},{5,7},{6,4},{7,5},{8,10},{9,11},{10,... | collective-permute-start | bytes 24584 | tf_op jit(solution)/shard_map/ppermute | solution.py:330
  21.1 5.7 %collective-permute-start.8 = (bf16[16,256]{1,0:T(8,128)(2,1)S(1)}, bf16[16,256]{1,0:T(8,128)(2,1)S(1)}, u32[]{:S(2)}, u32[]{:S(2)}) collective-permute-start(bf16[16,256]{1,0:T(8,128)(2,1)S(1)} %slice_bitcast_fusion.refs_2_), channel_id=1, source_target_pairs={{0,4},{1,5},{2,6},{3,7},{4,0},{5,1},{6,2},{7,3},{8,12},{9,13},{10,... | collective-permute-start | bytes 24584 | tf_op jit(solution)/shard_map/ppermute | solution.py:330
  23.7 5.4 %collective-permute-start.9 = (bf16[16,256]{1,0:T(8,128)(2,1)S(1)}, bf16[16,256]{1,0:T(8,128)(2,1)S(1)}, u32[]{:S(2)}, u32[]{:S(2)}) collective-permute-start(bf16[16,256]{1,0:T(8,128)(2,1)S(1)} %slice_bitcast_fusion.refs_2_), channel_id=1, source_target_pairs={{0,6},{1,7},{2,4},{3,5},{4,2},{5,3},{6,0},{7,1},{8,14},{9,15},{10,... | collective-permute-start | bytes 24584 | tf_op jit(solution)/shard_map/ppermute | solution.py:330
  26.9 8.1 %collective-permute-start.1 = (bf16[2,272,256]{2,1,0:T(8,128)(2,1)S(1)}, bf16[2,272,256]{2,1,0:T(8,128)(2,1)S(1)}, u32[]{:S(2)}, u32[]{:S(2)}) collective-permute-start(bf16[2,272,256]{2,1,0:T(8,128)(2,1)S(1)} %slice.12), channel_id=1, source_target_pairs={{0,16},{1,17},{2,18},{3,19},{4,20},{5,21},{6,22},{7,23},{8,24},{9,... | collective-permute-start | bytes 835592 | tf_op jit(solution)/shard_map/ppermute | solution.py:330
  29.2 7.4 %collective-permute-start.4 = (bf16[2,272,256]{2,1,0:T(8,128)(2,1)S(1)}, bf16[2,272,256]{2,1,0:T(8,128)(2,1)S(1)}, u32[]{:S(2)}, u32[]{:S(2)}) collective-permute-start(bf16[2,272,256]{2,1,0:T(8,128)(2,1)S(1)} %slice.13), channel_id=1, source_target_pairs={{0,1},{1,0},{2,3},{3,2},{4,5},{5,4},{6,7},{7,6},{8,9},{9,8},{10,11... | collective-permute-start | bytes 835592 | tf_op jit(solution)/shard_map/ppermute | solution.py:330
  35.0 14.1 %collective-permute-start.2 = (bf16[2,272,256]{2,1,0:T(8,128)(2,1)S(1)}, bf16[2,272,256]{2,1,0:T(8,128)(2,1)S(1)}, u32[]{:S(2)}, u32[]{:S(2)}) collective-permute-start(bf16[2,272,256]{2,1,0:T(8,128)(2,1)S(1)} %collective-permute-done.1.refs_0_), channel_id=1, source_target_pairs={{0,8},{1,9},{2,10},{3,11},{4,12},{5,13},{6,14},{7,15},{8,0},{9,1},... | collective-permute-start | bytes 835592 | tf_op jit(solution)/shard_map/ppermute | solution.py:330
  36.6 12.5 %collective-permute-start.5 = (bf16[2,272,256]{2,1,0:T(8,128)(2,1)S(1)}, bf16[2,272,256]{2,1,0:T(8,128)(2,1)S(1)}, u32[]{:S(2)}, u32[]{:S(2)}) collective-permute-start(bf16[2,272,256]{2,1,0:T(8,128)(2,1)S(1)} %collective-permute-done.4.refs_1_), channel_id=1, source_target_pairs={{0,8},{1,9},{2,10},{3,11},{4,12},{5,13},{6,14},{7,15},{8,0},{9,1},... | collective-permute-start | bytes 835592 | tf_op jit(solution)/shard_map/ppermute | solution.py:330
  49.0 15.9 %copy-start.1 = (s32[2,64]{1,0:T(2,128)S(1)}, s32[2,64]{1,0:T(2,128)}, u32[]{:S(2)}) copy-start(s32[2,64]{1,0:T(2,128)} %refs_5_.1) | copy-start | bytes 1540
  49.0 15.8 %copy-start.3 = (s32[1,64]{1,0:T(1,128)S(1)}, s32[1,64]{1,0:T(1,128)}, u32[]{:S(2)}) copy-start(s32[1,64]{1,0:T(1,128)} %refs_6_.1) | copy-start | bytes 772
  51.8 8.5 %collective-permute-start.12 = (bf16[256,256]{1,0:T(8,128)(2,1)S(1)}, bf16[256,256]{1,0:T(8,128)(2,1)S(1)}, u32[]{:S(2)}, u32[]{:S(2)}) collective-permute-start(bf16[256,256]{1,0:T(8,128)(2,1)S(1)} %get-tuple-element.19), channel_id=1, source_target_pairs={{0,2},{1,3},{2,0},{3,1},{4,6},{5,7},{6,4},{7,5},{8,10},{9,11},{10,... | collective-permute-start | bytes 393224 | tf_op jit(solution)/shard_map/ppermute | solution.py:330
  51.8 13.0 %collective-permute-start.13 = (bf16[256,256]{1,0:T(8,128)(2,1)S(1)}, bf16[256,256]{1,0:T(8,128)(2,1)S(1)}, u32[]{:S(2)}, u32[]{:S(2)}) collective-permute-start(bf16[256,256]{1,0:T(8,128)(2,1)S(1)} %get-tuple-element.20), channel_id=1, source_target_pairs={{0,4},{1,5},{2,6},{3,7},{4,0},{5,1},{6,2},{7,3},{8,12},{9,13},{10,... | collective-permute-start | bytes 393224 | tf_op jit(solution)/shard_map/ppermute | solution.py:330
  54.9 9.9 %collective-permute-start.14 = (bf16[256,256]{1,0:T(8,128)(2,1)S(1)}, bf16[256,256]{1,0:T(8,128)(2,1)S(1)}, u32[]{:S(2)}, u32[]{:S(2)}) collective-permute-start(bf16[256,256]{1,0:T(8,128)(2,1)S(1)} %get-tuple-element.21), channel_id=1, source_target_pairs={{0,6},{1,7},{2,4},{3,5},{4,2},{5,3},{6,0},{7,1},{8,14},{9,15},{10,... | collective-permute-start | bytes 393224 | tf_op jit(solution)/shard_map/ppermute | solution.py:330
  64.8 13.2 %copy-start = (s32[4,64]{1,0:T(4,128)S(1)}, s32[4,64]{1,0:T(4,128)}, u32[]{:S(2)}) copy-start(s32[4,64]{1,0:T(4,128)} %refs_3_.2) | copy-start | bytes 3076
  72.8 5.2 %collective-permute-start.15 = (f32[144,256]{1,0:T(8,128)S(1)}, f32[144,256]{1,0:T(8,128)S(1)}, u32[]{:S(2)}, u32[]{:S(2)}) collective-permute-start(f32[144,256]{1,0:T(8,128)S(1)} %get-tuple-element.23.refs_1_), channel_id=1, source_target_pairs={{0,1},{1,0},{2,3},{3,2},{4,5},{5,4},{6,7},{7,6},{8,9},{9,8},{10,11... | collective-permute-start | bytes 442376 | tf_op jit(solution)/shard_map/ppermute | solution.py:330
  73.8 14.4 %copy-start.2 = (s32[2,64]{1,0:T(2,128)S(1)}, s32[2,64]{1,0:T(2,128)}, u32[]{:S(2)}) copy-start(s32[2,64]{1,0:T(2,128)} %refs_3_.3) | copy-start | bytes 1540
  81.7 6.5 %collective-permute-start.16 = (f32[144,256]{1,0:T(8,128)S(1)}, f32[144,256]{1,0:T(8,128)S(1)}, u32[]{:S(2)}, u32[]{:S(2)}) collective-permute-start(f32[144,256]{1,0:T(8,128)S(1)} %get-tuple-element.24.refs_1_), channel_id=1, source_target_pairs={{0,2},{1,3},{2,0},{3,1},{4,6},{5,7},{6,4},{7,5},{8,10},{9,11},{10,... | collective-permute-start | bytes 442376 | tf_op jit(solution)/shard_map/ppermute | solution.py:330
